TPU v7x, 32 devices: a whole 2x2x4 slice. The times are simulated.
32 devices in a mesh: parts: 2 (over y), frame: 4 (over z), row: 4 (over x, core).
Axes of the slice: x: 2, y: 2, z: 4, core: 2. Of those that a mesh axis runs over, the one named last changes fastest.
Arguments:
- features: bfloat16 [4, 4, 32, 32, 128], P('parts', 'frame', 'row'), parts along dimension 0, may hold values from -6 to 6
- w_in: bfloat16 [2, 3, 3, 256, 128], replicated, as said below
- b_in: float32 [2, 128], replicated, may hold values from -3 to 3
- w_mid: bfloat16 [2, 3, 3, 128, 128], replicated, may hold values from -0.1875 to 0.1875
- b_mid: float32 [2, 128], replicated, may hold values from -3 to 3
- w_out: bfloat16 [2, 3, 3, 128, 128], replicated, may hold values from -0.1875 to 0.1875
- b_out: float32 [2, 128], replicated, may hold values from -3 to 3
Outputs:
- forward_states: bfloat16 [4, 4, 32, 32, 128], P('parts', 'frame', 'row'), parts along dimension 0
- backward_states: bfloat16 [4, 4, 32, 32, 128], P('parts', 'frame', 'row'), parts along dimension 0
There are 2 independent parts, one for each index of `parts`. A program takes and returns all parts, laid end to end along the dimension named above; an argument that names none is the same for every part. Nothing has to cross between parts.
Inputs may be any that keep to these rules, and one draw needn't show every extreme that they name: `w_in`: weights of the first convolutions.
All inputs are finite; a program needn't handle non-finite values.
Results may differ from a plain program's by a relative error of at most 0.014.
Values may be sent and summed in bfloat16 or wider, within the bound.
A program may use at most 64 MiB of HBM per device.

v0:
```python
import jax
import jax.numpy as jnp
from jax import lax
from jax.sharding import PartitionSpec as P


def with_halo(block, sides, width):
    for axis, dim in sides:
        count = lax.axis_size(axis)
        forward = [(i, i + 1) for i in range(count - 1)]
        backward = [(target, source) for source, target in forward]
        low = lax.ppermute(
            lax.slice_in_dim(block, block.shape[dim] - width, None, axis=dim), axis, forward
        )
        high = lax.ppermute(lax.slice_in_dim(block, 0, width, axis=dim), axis, backward)
        block = jnp.concatenate([low, block, high], axis=dim)
    return block


def shifted(shard, axis, by):
    length = lax.axis_size(axis)
    pairs = [(i, i + by) for i in range(length) if 0 <= i + by < length]
    return lax.ppermute(shard, axis, pairs)


def conv_layer(field, weight, bias_vec):
    padded = jnp.pad(field, ((0, 0), (1, 1), (0, 0)))
    row_count = padded.shape[0] - 2
    col_count = padded.shape[1] - 2
    summed = jnp.zeros((row_count, col_count, weight.shape[-1]), jnp.float32)
    for offset_y in range(3):
        for offset_x in range(3):
            window = padded[offset_y : offset_y + row_count, offset_x : offset_x + col_count, :]
            product = jnp.dot(
                window.reshape(row_count * col_count, window.shape[-1]),
                weight[offset_y, offset_x],
                preferred_element_type=jnp.float32,
            )
            summed = summed + product.reshape(row_count, col_count, weight.shape[-1])
    return summed + bias_vec


def activate(values):
    return jax.nn.gelu(values, approximate=False)


def on_device(features, w_in, b_in, w_mid, b_mid, w_out, b_out):
    clip_count, frame_count, row_count, col_count, channels = features.shape
    owners = lax.axis_size("frame")
    owner_pos = lax.axis_index("frame")
    section_total = owners + clip_count - 1
    rim_depth = 3
    rimmed = with_halo(features, (("row", 2),), rim_depth)
    slab_start = lax.axis_index("row") * row_count
    total_rows = row_count * lax.axis_size("row")
    outer_rows = slab_start - 2 + jnp.arange(row_count + 4, dtype=jnp.int32)
    outer_mask = ((outer_rows >= 0) & (outer_rows < total_rows)).astype(jnp.float32)[:, None, None]
    inner_rows = slab_start - 1 + jnp.arange(row_count + 2, dtype=jnp.int32)
    inner_mask = ((inner_rows >= 0) & (inner_rows < total_rows)).astype(jnp.float32)[:, None, None]
    zero_state = jnp.zeros((row_count, col_count, channels), jnp.bfloat16)

    def skipped(operand):
        return zero_state

    def frame_step(frame_rim, carried, direction, is_live):
        state_rim = with_halo(carried, (("row", 0),), rim_depth)
        joined = jnp.concatenate([frame_rim, state_rim], axis=-1)

        def compute(joined_in):
            first_act = (
                activate(conv_layer(joined_in, w_in[direction], b_in[direction])) * outer_mask
            ).astype(jnp.bfloat16)
            middle = (
                activate(conv_layer(first_act, w_mid[direction], b_mid[direction])) * inner_mask
            ).astype(jnp.bfloat16)
            residual = first_act[2:-2].astype(jnp.float32)
            return (residual + conv_layer(middle, w_out[direction], b_out[direction])).astype(
                jnp.bfloat16
            )

        return lax.cond(is_live, compute, skipped, joined)

    def sweep_section(section_num, incoming, outputs, direction):
        position = owner_pos if direction == 0 else owners - 1 - owner_pos
        clip_index = section_num - position
        is_live = (clip_index >= 0) & (clip_index < clip_count)
        chosen = jnp.clip(clip_index, 0, clip_count - 1)
        clip_frames = lax.dynamic_index_in_dim(rimmed, chosen, 0, keepdims=False)
        clip_out = lax.dynamic_index_in_dim(outputs, chosen, 0, keepdims=False)
        carried = incoming
        frame_order = range(frame_count) if direction == 0 else range(frame_count - 1, -1, -1)
        for frame_slot in frame_order:
            carried = frame_step(clip_frames[frame_slot], carried, direction, is_live)
            clip_out = clip_out.at[frame_slot].set(
                jnp.where(is_live, carried, clip_out[frame_slot])
            )
        outputs = lax.dynamic_update_index_in_dim(outputs, clip_out, chosen, 0)
        if direction == 0:
            passed = shifted(carried, "frame", 1)
        else:
            passed = shifted(carried, "frame", -1)
        return (passed, outputs)

    blank_out = jnp.zeros_like(features)

    def forward_turn(section_num, carry):
        return sweep_section(section_num, carry[0], carry[1], 0)

    def backward_turn(section_num, carry):
        return sweep_section(section_num, carry[0], carry[1], 1)

    _, forward_states = lax.fori_loop(0, section_total, forward_turn, (zero_state, blank_out))
    _, backward_states = lax.fori_loop(0, section_total, backward_turn, (zero_state, blank_out))
    return (forward_states, backward_states)


def solution(mesh):
    placed = (P("parts", "frame", "row", None, None), P(), P(), P(), P(), P(), P())
    return jax.shard_map(
        on_device,
        mesh=mesh,
        in_specs=placed,
        out_specs=(P("parts", "frame", "row", None, None), P("parts", "frame", "row", None, None)),
        check_vma=False,
    )
```

profile of v0, /device:TPU:26, one launch (start us, length us, event | category | flops | bytes accessed | tf_op | source)
XLA Modules:
  0.0 211.5 jit_solution(961536091696717893)
XLA Ops:
  0.6 0.8 fusion.166
  1.5 1.9 collective-permute-start.6
  3.4 3.6 %collective-permute-start.7 = (bf16[2,1,3,32,128]{4,3,2,1,0:T(8,128)(2,1)S(1)}, bf16[2,1,3,32,128]{4,3,2,1,0:T(8,128)(2,1)S(1)}, u32[]{:S(2)}, u32[]{:S(2)}) collective-permute-start(bf16[2,1,3,32,128]{4,3,2,1,0:T(8,128)(2,1)S(1)} %get-tuple-element.936), channel_id=1, source_target_pairs={{1,0},{2,1},{3,2},{5,4},{6,5},{7,6},{9,8},{10,9},{11,10},{13,12},{... | collective-permute-start | bytes 147464 | tf_op jit(solution)/shard_map/ppermute | solution.py:15
  7.1 0.9 constant_dynamic-update-slice_fusion.1
  8.8 92.5 %while.41 = (s32[]{:T(128)}, bf16[8,32,128]{2,1,0:T(8,128)(2,1)S(1)}, bf16[2,1,8,32,128]{4,3,2,1,0:T(8,128)(2,1)S(1)}, s32[]{:T(128)}, bf16[2,1,14,32,128]{4,3,2...) while((s32[]{:T(128)}, ...), condition=%wide.region_7.8_spmd.clone, body=%wide.region_4.7_spmd.clone.sunk | while | flops 404463744 | bytes 21710996 | solution.py:113
  8.8 3.7 %collective-permute-start.3 = (bf16[3,32,128]{2,1,0:T(8,128)(2,1)S(1)}, bf16[3,32,128]{2,1,0:T(8,128)(2,1)S(1)}, u32[]{:S(2)}, u32[]{:S(2)}) collective-permute-start(bf16[3,32,128]{2,1,0:T(8,128)(2,1)S(1)} %get-tuple-element.1102), channel_id=1, source_target_pairs={{1,0},{2,1},{3,2},{5,4},{6,5},{7,6},{9,8},{10,9},{11,10},{13,12},{... | collective-permute-start | bytes 73736 | tf_op jit(solution)/shard_map/while/body/eval_jaxpr/ppermute | solution.py:15
  12.5 1.9 collective-permute-start.4
  14.6 3.1 %collective-permute-done.4 = bf16[3,32,128]{2,1,0:T(8,128)(2,1)S(1)} collective-permute-done((bf16[3,32,128]{2,1,0:T(8,128)(2,1)S(1)}, bf16[3,32,128]{2,1,0:T(8,128)(2,1)S(1)}, u32[]{:S(2)}, u32[]{:S(2)}) %collective-permute-start.4) | collective-permute-done | bytes 24608 | tf_op jit(solution)/shard_map/while/body/eval_jaxpr/ppermute | solution.py:12
  17.7 7.4 %conditional.7 = (bf16[8,32,128]{2,1,0:T(8,128)(2,1)S(1)}) conditional(s32[]{:T(128)} %convert_element_type.118, () %tuple.132, (bf16[14,32,256]{2,1,0:T(8,128)(2,1)S(1)}, bf16[2,3,3,256,128]{4,3,2,1,0:T(8,128)(2,1)}, f32[2,128]{1,0:T(2,128)}, f32[12,1,1]{0,2,1:T(1,128)S(1)}, bf16[2,3,3,128,128]{4,3,2,1,0:T(8,128)(2,1)}, ...), branch_computations={%region_5.5_spmd, %region_6.6_spmd} | conditional | flops 403513344 | bytes 20137620 | solution.py:81
  17.7 1.1 slice_bitcast_fusion.60
  25.1 1.3 collective-permute-start.5
  26.5 1.8 collective-permute-done.5
  28.3 1.9 collective-permute-start.3
  30.2 2.4 %collective-permute-start.4 = (bf16[3,32,128]{2,1,0:T(8,128)(2,1)S(1)}, bf16[3,32,128]{2,1,0:T(8,128)(2,1)S(1)}, u32[]{:S(2)}, u32[]{:S(2)}) collective-permute-start(bf16[3,32,128]{2,1,0:T(8,128)(2,1)S(1)} %get-tuple-element.1103), channel_id=1, source_target_pairs={{0,1},{1,2},{2,3},{4,5},{5,6},{6,7},{8,9},{9,10},{10,11},{12,13},{... | collective-permute-start | bytes 73736 | tf_op jit(solution)/shard_map/while/body/eval_jaxpr/ppermute | solution.py:12
  32.8 2.6 %collective-permute-done.4 = bf16[3,32,128]{2,1,0:T(8,128)(2,1)S(1)} collective-permute-done((bf16[3,32,128]{2,1,0:T(8,128)(2,1)S(1)}, bf16[3,32,128]{2,1,0:T(8,128)(2,1)S(1)}, u32[]{:S(2)}, u32[]{:S(2)}) %collective-permute-start.4) | collective-permute-done | bytes 24608 | tf_op jit(solution)/shard_map/while/body/eval_jaxpr/ppermute | solution.py:12
  35.4 7.4 %conditional.7 = (bf16[8,32,128]{2,1,0:T(8,128)(2,1)S(1)}) conditional(s32[]{:T(128)} %convert_element_type.118, () %tuple.132, (bf16[14,32,256]{2,1,0:T(8,128)(2,1)S(1)}, bf16[2,3,3,256,128]{4,3,2,1,0:T(8,128)(2,1)}, f32[2,128]{1,0:T(2,128)}, f32[12,1,1]{0,2,1:T(1,128)S(1)}, bf16[2,3,3,128,128]{4,3,2,1,0:T(8,128)(2,1)}, ...), branch_computations={%region_5.5_spmd, %region_6.6_spmd} | conditional | flops 403513344 | bytes 20137620 | solution.py:81
  35.4 1.1 slice_bitcast_fusion.60
  42.9 4.3 %collective-permute-start.5 = (bf16[8,32,128]{2,1,0:T(8,128)(2,1)S(1)}, bf16[8,32,128]{2,1,0:T(8,128)(2,1)S(1)}, u32[]{:S(2)}, u32[]{:S(2)}) collective-permute-start(bf16[8,32,128]{2,1,0:T(8,128)(2,1)S(1)} %get-tuple-element.1201), channel_id=1, source_target_pairs={{4,0},{8,4},{12,8},{5,1},{9,5},{13,9},{6,2},{10,6},{14,10},{7,3},{... | collective-permute-start | bytes 196616 | tf_op jit(solution)/shard_map/while/body/eval_jaxpr/ppermute | solution.py:23
  47.2 1.8 collective-permute-done.5
  49.0 1.9 collective-permute-start.3
  50.9 2.4 %collective-permute-start.4 = (bf16[3,32,128]{2,1,0:T(8,128)(2,1)S(1)}, bf16[3,32,128]{2,1,0:T(8,128)(2,1)S(1)}, u32[]{:S(2)}, u32[]{:S(2)}) collective-permute-start(bf16[3,32,128]{2,1,0:T(8,128)(2,1)S(1)} %get-tuple-element.1103), channel_id=1, source_target_pairs={{0,1},{1,2},{2,3},{4,5},{5,6},{6,7},{8,9},{9,10},{10,11},{12,13},{... | collective-permute-start | bytes 73736 | tf_op jit(solution)/shard_map/while/body/eval_jaxpr/ppermute | solution.py:12
  53.4 2.6 %collective-permute-done.4 = bf16[3,32,128]{2,1,0:T(8,128)(2,1)S(1)} collective-permute-done((bf16[3,32,128]{2,1,0:T(8,128)(2,1)S(1)}, bf16[3,32,128]{2,1,0:T(8,128)(2,1)S(1)}, u32[]{:S(2)}, u32[]{:S(2)}) %collective-permute-start.4) | collective-permute-done | bytes 24608 | tf_op jit(solution)/shard_map/while/body/eval_jaxpr/ppermute | solution.py:12
  56.2 11.7 %collective-permute-start.5 = (bf16[8,32,128]{2,1,0:T(8,128)(2,1)S(1)}, bf16[8,32,128]{2,1,0:T(8,128)(2,1)S(1)}, u32[]{:S(2)}, u32[]{:S(2)}) collective-permute-start(bf16[8,32,128]{2,1,0:T(8,128)(2,1)S(1)} %get-tuple-element.1201), channel_id=1, source_target_pairs={{4,0},{8,4},{12,8},{5,1},{9,5},{13,9},{6,2},{10,6},{14,10},{7,3},{... | collective-permute-start | bytes 196616 | tf_op jit(solution)/shard_map/while/body/eval_jaxpr/ppermute | solution.py:23
  67.9 1.8 collective-permute-done.5
  69.7 1.9 collective-permute-start.3
  71.6 2.4 %collective-permute-start.4 = (bf16[3,32,128]{2,1,0:T(8,128)(2,1)S(1)}, bf16[3,32,128]{2,1,0:T(8,128)(2,1)S(1)}, u32[]{:S(2)}, u32[]{:S(2)}) collective-permute-start(bf16[3,32,128]{2,1,0:T(8,128)(2,1)S(1)} %get-tuple-element.1103), channel_id=1, source_target_pairs={{0,1},{1,2},{2,3},{4,5},{5,6},{6,7},{8,9},{9,10},{10,11},{12,13},{... | collective-permute-start | bytes 73736 | tf_op jit(solution)/shard_map/while/body/eval_jaxpr/ppermute | solution.py:12
  74.1 2.6 %collective-permute-done.4 = bf16[3,32,128]{2,1,0:T(8,128)(2,1)S(1)} collective-permute-done((bf16[3,32,128]{2,1,0:T(8,128)(2,1)S(1)}, bf16[3,32,128]{2,1,0:T(8,128)(2,1)S(1)}, u32[]{:S(2)}, u32[]{:S(2)}) %collective-permute-start.4) | collective-permute-done | bytes 24608 | tf_op jit(solution)/shard_map/while/body/eval_jaxpr/ppermute | solution.py:12
  76.8 4.3 %collective-permute-start.5 = (bf16[8,32,128]{2,1,0:T(8,128)(2,1)S(1)}, bf16[8,32,128]{2,1,0:T(8,128)(2,1)S(1)}, u32[]{:S(2)}, u32[]{:S(2)}) collective-permute-start(bf16[8,32,128]{2,1,0:T(8,128)(2,1)S(1)} %get-tuple-element.1201), channel_id=1, source_target_pairs={{4,0},{8,4},{12,8},{5,1},{9,5},{13,9},{6,2},{10,6},{14,10},{7,3},{... | collective-permute-start | bytes 196616 | tf_op jit(solution)/shard_map/while/body/eval_jaxpr/ppermute | solution.py:23
  81.2 1.8 collective-permute-done.5
  83.0 1.9 collective-permute-start.3
  84.9 2.4 %collective-permute-start.4 = (bf16[3,32,128]{2,1,0:T(8,128)(2,1)S(1)}, bf16[3,32,128]{2,1,0:T(8,128)(2,1)S(1)}, u32[]{:S(2)}, u32[]{:S(2)}) collective-permute-start(bf16[3,32,128]{2,1,0:T(8,128)(2,1)S(1)} %get-tuple-element.1103), channel_id=1, source_target_pairs={{0,1},{1,2},{2,3},{4,5},{5,6},{6,7},{8,9},{9,10},{10,11},{12,13},{... | collective-permute-start | bytes 73736 | tf_op jit(solution)/shard_map/while/body/eval_jaxpr/ppermute | solution.py:12
  87.4 2.6 %collective-permute-done.4 = bf16[3,32,128]{2,1,0:T(8,128)(2,1)S(1)} collective-permute-done((bf16[3,32,128]{2,1,0:T(8,128)(2,1)S(1)}, bf16[3,32,128]{2,1,0:T(8,128)(2,1)S(1)}, u32[]{:S(2)}, u32[]{:S(2)}) %collective-permute-start.4) | collective-permute-done | bytes 24608 | tf_op jit(solution)/shard_map/while/body/eval_jaxpr/ppermute | solution.py:12
  90.2 9.3 %collective-permute-start.5 = (bf16[8,32,128]{2,1,0:T(8,128)(2,1)S(1)}, bf16[8,32,128]{2,1,0:T(8,128)(2,1)S(1)}, u32[]{:S(2)}, u32[]{:S(2)}) collective-permute-start(bf16[8,32,128]{2,1,0:T(8,128)(2,1)S(1)} %get-tuple-element.1201), channel_id=1, source_target_pairs={{4,0},{8,4},{12,8},{5,1},{9,5},{13,9},{6,2},{10,6},{14,10},{7,3},{... | collective-permute-start | bytes 196616 | tf_op jit(solution)/shard_map/while/body/eval_jaxpr/ppermute | solution.py:23
  99.5 1.8 collective-permute-done.5
  102.0 108.9 %while.40 = (s32[]{:T(128)}, bf16[8,32,128]{2,1,0:T(8,128)(2,1)S(1)}, bf16[2,1,8,32,128]{4,3,2,1,0:T(8,128)(2,1)S(1)}, s32[]{:T(128)}, bf16[2,1,14,32,128]{4,3,2...) while((s32[]{:T(128)}, ...), condition=%wide.region_3.4_spmd.clone, body=%wide.region_0.3_spmd.clone.sunk | while | flops 404463744 | bytes 21710996 | solution.py:112
  102.0 1.9 collective-permute-start
  103.9 2.4 %collective-permute-start.1 = (bf16[3,32,128]{2,1,0:T(8,128)(2,1)S(1)}, bf16[3,32,128]{2,1,0:T(8,128)(2,1)S(1)}, u32[]{:S(2)}, u32[]{:S(2)}) collective-permute-start(bf16[3,32,128]{2,1,0:T(8,128)(2,1)S(1)} %get-tuple-element.1088), channel_id=1, source_target_pairs={{0,1},{1,2},{2,3},{4,5},{5,6},{6,7},{8,9},{9,10},{10,11},{12,13},{... | collective-permute-start | bytes 73736 | tf_op jit(solution)/shard_map/while/body/eval_jaxpr/ppermute | solution.py:12
  106.4 2.6 %collective-permute-done.1 = bf16[3,32,128]{2,1,0:T(8,128)(2,1)S(1)} collective-permute-done((bf16[3,32,128]{2,1,0:T(8,128)(2,1)S(1)}, bf16[3,32,128]{2,1,0:T(8,128)(2,1)S(1)}, u32[]{:S(2)}, u32[]{:S(2)}) %collective-permute-start.1) | collective-permute-done | bytes 24608 | tf_op jit(solution)/shard_map/while/body/eval_jaxpr/ppermute | solution.py:12
  109.2 1.3 collective-permute-start.2
  110.5 5.2 %collective-permute-done.2 = bf16[8,32,128]{2,1,0:T(8,128)(2,1)S(1)} collective-permute-done((bf16[8,32,128]{2,1,0:T(8,128)(2,1)S(1)}, bf16[8,32,128]{2,1,0:T(8,128)(2,1)S(1)}, u32[]{:S(2)}, u32[]{:S(2)}) %collective-permute-start.2) | collective-permute-done | bytes 65568 | tf_op jit(solution)/shard_map/while/body/eval_jaxpr/ppermute | solution.py:23
  115.7 1.9 collective-permute-start
  117.6 2.4 %collective-permute-start.1 = (bf16[3,32,128]{2,1,0:T(8,128)(2,1)S(1)}, bf16[3,32,128]{2,1,0:T(8,128)(2,1)S(1)}, u32[]{:S(2)}, u32[]{:S(2)}) collective-permute-start(bf16[3,32,128]{2,1,0:T(8,128)(2,1)S(1)} %get-tuple-element.1088), channel_id=1, source_target_pairs={{0,1},{1,2},{2,3},{4,5},{5,6},{6,7},{8,9},{9,10},{10,11},{12,13},{... | collective-permute-start | bytes 73736 | tf_op jit(solution)/shard_map/while/body/eval_jaxpr/ppermute | solution.py:12
  120.1 2.6 %collective-permute-done.1 = bf16[3,32,128]{2,1,0:T(8,128)(2,1)S(1)} collective-permute-done((bf16[3,32,128]{2,1,0:T(8,128)(2,1)S(1)}, bf16[3,32,128]{2,1,0:T(8,128)(2,1)S(1)}, u32[]{:S(2)}, u32[]{:S(2)}) %collective-permute-start.1) | collective-permute-done | bytes 24608 | tf_op jit(solution)/shard_map/while/body/eval_jaxpr/ppermute | solution.py:12
  122.8 1.3 collective-permute-start.2
  124.1 10.2 %collective-permute-done.2 = bf16[8,32,128]{2,1,0:T(8,128)(2,1)S(1)} collective-permute-done((bf16[8,32,128]{2,1,0:T(8,128)(2,1)S(1)}, bf16[8,32,128]{2,1,0:T(8,128)(2,1)S(1)}, u32[]{:S(2)}, u32[]{:S(2)}) %collective-permute-start.2) | collective-permute-done | bytes 65568 | tf_op jit(solution)/shard_map/while/body/eval_jaxpr/ppermute | solution.py:23
  134.3 1.9 collective-permute-start
  136.3 2.4 %collective-permute-start.1 = (bf16[3,32,128]{2,1,0:T(8,128)(2,1)S(1)}, bf16[3,32,128]{2,1,0:T(8,128)(2,1)S(1)}, u32[]{:S(2)}, u32[]{:S(2)}) collective-permute-start(bf16[3,32,128]{2,1,0:T(8,128)(2,1)S(1)} %get-tuple-element.1088), channel_id=1, source_target_pairs={{0,1},{1,2},{2,3},{4,5},{5,6},{6,7},{8,9},{9,10},{10,11},{12,13},{... | collective-permute-start | bytes 73736 | tf_op jit(solution)/shard_map/while/body/eval_jaxpr/ppermute | solution.py:12
  138.8 2.6 %collective-permute-done.1 = bf16[3,32,128]{2,1,0:T(8,128)(2,1)S(1)} collective-permute-done((bf16[3,32,128]{2,1,0:T(8,128)(2,1)S(1)}, bf16[3,32,128]{2,1,0:T(8,128)(2,1)S(1)}, u32[]{:S(2)}, u32[]{:S(2)}) %collective-permute-start.1) | collective-permute-done | bytes 24608 | tf_op jit(solution)/shard_map/while/body/eval_jaxpr/ppermute | solution.py:12
  141.5 1.3 collective-permute-start.2
  142.8 26.7 %collective-permute-done.2 = bf16[8,32,128]{2,1,0:T(8,128)(2,1)S(1)} collective-permute-done((bf16[8,32,128]{2,1,0:T(8,128)(2,1)S(1)}, bf16[8,32,128]{2,1,0:T(8,128)(2,1)S(1)}, u32[]{:S(2)}, u32[]{:S(2)}) %collective-permute-start.2) | collective-permute-done | bytes 65568 | tf_op jit(solution)/shard_map/while/body/eval_jaxpr/ppermute | solution.py:23
  169.5 1.9 collective-permute-start
  171.4 2.4 %collective-permute-start.1 = (bf16[3,32,128]{2,1,0:T(8,128)(2,1)S(1)}, bf16[3,32,128]{2,1,0:T(8,128)(2,1)S(1)}, u32[]{:S(2)}, u32[]{:S(2)}) collective-permute-start(bf16[3,32,128]{2,1,0:T(8,128)(2,1)S(1)} %get-tuple-element.1088), channel_id=1, source_target_pairs={{0,1},{1,2},{2,3},{4,5},{5,6},{6,7},{8,9},{9,10},{10,11},{12,13},{... | collective-permute-start | bytes 73736 | tf_op jit(solution)/shard_map/while/body/eval_jaxpr/ppermute | solution.py:12
  173.9 2.6 %collective-permute-done.1 = bf16[3,32,128]{2,1,0:T(8,128)(2,1)S(1)} collective-permute-done((bf16[3,32,128]{2,1,0:T(8,128)(2,1)S(1)}, bf16[3,32,128]{2,1,0:T(8,128)(2,1)S(1)}, u32[]{:S(2)}, u32[]{:S(2)}) %collective-permute-start.1) | collective-permute-done | bytes 24608 | tf_op jit(solution)/shard_map/while/body/eval_jaxpr/ppermute | solution.py:12
  176.6 7.4 %conditional.6 = (bf16[8,32,128]{2,1,0:T(8,128)(2,1)S(1)}) conditional(s32[]{:T(128)} %convert_element_type.115, () %tuple.128, (bf16[14,32,256]{2,1,0:T(8,128)(2,1)S(1)}, bf16[2,3,3,256,128]{4,3,2,1,0:T(8,128)(2,1)}, f32[2,128]{1,0:T(2,128)}, f32[12,1,1]{0,2,1:T(1,128)S(1)}, bf16[2,3,3,128,128]{4,3,2,1,0:T(8,128)(2,1)}, ...), branch_computations={%region_1.1_spmd, %region_2.2_spmd} | conditional | flops 403513344 | bytes 20137620 | solution.py:81
  176.6 1.1 slice_bitcast_fusion
  184.0 1.3 collective-permute-start.2
  185.4 4.8 %collective-permute-done.2 = bf16[8,32,128]{2,1,0:T(8,128)(2,1)S(1)} collective-permute-done((bf16[8,32,128]{2,1,0:T(8,128)(2,1)S(1)}, bf16[8,32,128]{2,1,0:T(8,128)(2,1)S(1)}, u32[]{:S(2)}, u32[]{:S(2)}) %collective-permute-start.2) | collective-permute-done | bytes 65568 | tf_op jit(solution)/shard_map/while/body/eval_jaxpr/ppermute | solution.py:23
  190.2 1.9 collective-permute-start
  192.1 2.4 %collective-permute-start.1 = (bf16[3,32,128]{2,1,0:T(8,128)(2,1)S(1)}, bf16[3,32,128]{2,1,0:T(8,128)(2,1)S(1)}, u32[]{:S(2)}, u32[]{:S(2)}) collective-permute-start(bf16[3,32,128]{2,1,0:T(8,128)(2,1)S(1)} %get-tuple-element.1088), channel_id=1, source_target_pairs={{0,1},{1,2},{2,3},{4,5},{5,6},{6,7},{8,9},{9,10},{10,11},{12,13},{... | collective-permute-start | bytes 73736 | tf_op jit(solution)/shard_map/while/body/eval_jaxpr/ppermute | solution.py:12
  194.6 2.6 %collective-permute-done.1 = bf16[3,32,128]{2,1,0:T(8,128)(2,1)S(1)} collective-permute-done((bf16[3,32,128]{2,1,0:T(8,128)(2,1)S(1)}, bf16[3,32,128]{2,1,0:T(8,128)(2,1)S(1)}, u32[]{:S(2)}, u32[]{:S(2)}) %collective-permute-start.1) | collective-permute-done | bytes 24608 | tf_op jit(solution)/shard_map/while/body/eval_jaxpr/ppermute | solution.py:12
  197.3 7.4 %conditional.6 = (bf16[8,32,128]{2,1,0:T(8,128)(2,1)S(1)}) conditional(s32[]{:T(128)} %convert_element_type.115, () %tuple.128, (bf16[14,32,256]{2,1,0:T(8,128)(2,1)S(1)}, bf16[2,3,3,256,128]{4,3,2,1,0:T(8,128)(2,1)}, f32[2,128]{1,0:T(2,128)}, f32[12,1,1]{0,2,1:T(1,128)S(1)}, bf16[2,3,3,128,128]{4,3,2,1,0:T(8,128)(2,1)}, ...), branch_computations={%region_1.1_spmd, %region_2.2_spmd} | conditional | flops 403513344 | bytes 20137620 | solution.py:81
  197.3 1.1 slice_bitcast_fusion
  204.7 1.3 collective-permute-start.2
  206.0 4.8 %collective-permute-done.2 = bf16[8,32,128]{2,1,0:T(8,128)(2,1)S(1)} collective-permute-done((bf16[8,32,128]{2,1,0:T(8,128)(2,1)S(1)}, bf16[8,32,128]{2,1,0:T(8,128)(2,1)S(1)}, u32[]{:S(2)}, u32[]{:S(2)}) %collective-permute-start.2) | collective-permute-done | bytes 65568 | tf_op jit(solution)/shard_map/while/body/eval_jaxpr/ppermute | solution.py:23
  (264 shorter events, 27.8 us)
Async XLA Ops:
  1.5 5.6 %collective-permute-start.6 = (bf16[2,1,3,32,128]{4,3,2,1,0:T(8,128)(2,1)S(1)}, bf16[2,1,3,32,128]{4,3,2,1,0:T(8,128)(2,1)S(1)}, u32[]{:S(2)}, u32[]{:S(2)}) collective-permute-start(bf16[2,1,3,32,128]{4,3,2,1,0:T(8,128)(2,1)S(1)} %get-tuple-element.937), channel_id=1, source_target_pairs={{0,1},{1,2},{2,3},{4,5},{5,6},{6,7},{8,9},{9,10},{10,11},{12,13},{... | collective-permute-start | bytes 147464 | tf_op jit(solution)/shard_map/ppermute | solution.py:12
  3.4 5.4 %collective-permute-start.7 = (bf16[2,1,3,32,128]{4,3,2,1,0:T(8,128)(2,1)S(1)}, bf16[2,1,3,32,128]{4,3,2,1,0:T(8,128)(2,1)S(1)}, u32[]{:S(2)}, u32[]{:S(2)}) collective-permute-start(bf16[2,1,3,32,128]{4,3,2,1,0:T(8,128)(2,1)S(1)} %get-tuple-element.936), channel_id=1, source_target_pairs={{1,0},{2,1},{3,2},{5,4},{6,5},{7,6},{9,8},{10,9},{11,10},{13,12},{... | collective-permute-start | bytes 147464 | tf_op jit(solution)/shard_map/ppermute | solution.py:15
  8.8 5.7 %collective-permute-start.3 = (bf16[3,32,128]{2,1,0:T(8,128)(2,1)S(1)}, bf16[3,32,128]{2,1,0:T(8,128)(2,1)S(1)}, u32[]{:S(2)}, u32[]{:S(2)}) collective-permute-start(bf16[3,32,128]{2,1,0:T(8,128)(2,1)S(1)} %get-tuple-element.1102), channel_id=1, source_target_pairs={{1,0},{2,1},{3,2},{5,4},{6,5},{7,6},{9,8},{10,9},{11,10},{13,12},{... | collective-permute-start | bytes 73736 | tf_op jit(solution)/shard_map/while/body/eval_jaxpr/ppermute | solution.py:15
  12.5 5.1 %collective-permute-start.4 = (bf16[3,32,128]{2,1,0:T(8,128)(2,1)S(1)}, bf16[3,32,128]{2,1,0:T(8,128)(2,1)S(1)}, u32[]{:S(2)}, u32[]{:S(2)}) collective-permute-start(bf16[3,32,128]{2,1,0:T(8,128)(2,1)S(1)} %get-tuple-element.1103), channel_id=1, source_target_pairs={{0,1},{1,2},{2,3},{4,5},{5,6},{6,7},{8,9},{9,10},{10,11},{12,13},{... | collective-permute-start | bytes 73736 | tf_op jit(solution)/shard_map/while/body/eval_jaxpr/ppermute | solution.py:12
  19.7 0.9 copy-start.10
  20.6 1.1 copy-start
  20.6 1.2 copy-start.2
  22.4 0.8 copy-start.6
  22.4 0.8 copy-start.8
  25.1 3.2 %collective-permute-start.5 = (bf16[8,32,128]{2,1,0:T(8,128)(2,1)S(1)}, bf16[8,32,128]{2,1,0:T(8,128)(2,1)S(1)}, u32[]{:S(2)}, u32[]{:S(2)}) collective-permute-start(bf16[8,32,128]{2,1,0:T(8,128)(2,1)S(1)} %get-tuple-element.1201), channel_id=1, source_target_pairs={{4,0},{8,4},{12,8},{5,1},{9,5},{13,9},{6,2},{10,6},{14,10},{7,3},{... | collective-permute-start | bytes 196616 | tf_op jit(solution)/shard_map/while/body/eval_jaxpr/ppermute | solution.py:23
  28.3 4.4 %collective-permute-start.3 = (bf16[3,32,128]{2,1,0:T(8,128)(2,1)S(1)}, bf16[3,32,128]{2,1,0:T(8,128)(2,1)S(1)}, u32[]{:S(2)}, u32[]{:S(2)}) collective-permute-start(bf16[3,32,128]{2,1,0:T(8,128)(2,1)S(1)} %get-tuple-element.1102), channel_id=1, source_target_pairs={{1,0},{2,1},{3,2},{5,4},{6,5},{7,6},{9,8},{10,9},{11,10},{13,12},{... | collective-permute-start | bytes 73736 | tf_op jit(solution)/shard_map/while/body/eval_jaxpr/ppermute | solution.py:15
  30.2 5.1 %collective-permute-start.4 = (bf16[3,32,128]{2,1,0:T(8,128)(2,1)S(1)}, bf16[3,32,128]{2,1,0:T(8,128)(2,1)S(1)}, u32[]{:S(2)}, u32[]{:S(2)}) collective-permute-start(bf16[3,32,128]{2,1,0:T(8,128)(2,1)S(1)} %get-tuple-element.1103), channel_id=1, source_target_pairs={{0,1},{1,2},{2,3},{4,5},{5,6},{6,7},{8,9},{9,10},{10,11},{12,13},{... | collective-permute-start | bytes 73736 | tf_op jit(solution)/shard_map/while/body/eval_jaxpr/ppermute | solution.py:12
  37.4 0.9 copy-start.10
  38.3 1.1 copy-start
  38.3 1.2 copy-start.2
  40.1 0.8 copy-start.6
  40.1 0.8 copy-start.8
  42.9 6.2 %collective-permute-start.5 = (bf16[8,32,128]{2,1,0:T(8,128)(2,1)S(1)}, bf16[8,32,128]{2,1,0:T(8,128)(2,1)S(1)}, u32[]{:S(2)}, u32[]{:S(2)}) collective-permute-start(bf16[8,32,128]{2,1,0:T(8,128)(2,1)S(1)} %get-tuple-element.1201), channel_id=1, source_target_pairs={{4,0},{8,4},{12,8},{5,1},{9,5},{13,9},{6,2},{10,6},{14,10},{7,3},{... | collective-permute-start | bytes 196616 | tf_op jit(solution)/shard_map/while/body/eval_jaxpr/ppermute | solution.py:23
  49.0 4.4 %collective-permute-start.3 = (bf16[3,32,128]{2,1,0:T(8,128)(2,1)S(1)}, bf16[3,32,128]{2,1,0:T(8,128)(2,1)S(1)}, u32[]{:S(2)}, u32[]{:S(2)}) collective-permute-start(bf16[3,32,128]{2,1,0:T(8,128)(2,1)S(1)} %get-tuple-element.1102), channel_id=1, source_target_pairs={{1,0},{2,1},{3,2},{5,4},{6,5},{7,6},{9,8},{10,9},{11,10},{13,12},{... | collective-permute-start | bytes 73736 | tf_op jit(solution)/shard_map/while/body/eval_jaxpr/ppermute | solution.py:15
  50.9 5.1 %collective-permute-start.4 = (bf16[3,32,128]{2,1,0:T(8,128)(2,1)S(1)}, bf16[3,32,128]{2,1,0:T(8,128)(2,1)S(1)}, u32[]{:S(2)}, u32[]{:S(2)}) collective-permute-start(bf16[3,32,128]{2,1,0:T(8,128)(2,1)S(1)} %get-tuple-element.1103), channel_id=1, source_target_pairs={{0,1},{1,2},{2,3},{4,5},{5,6},{6,7},{8,9},{9,10},{10,11},{12,13},{... | collective-permute-start | bytes 73736 | tf_op jit(solution)/shard_map/while/body/eval_jaxpr/ppermute | solution.py:12
  56.2 13.5 %collective-permute-start.5 = (bf16[8,32,128]{2,1,0:T(8,128)(2,1)S(1)}, bf16[8,32,128]{2,1,0:T(8,128)(2,1)S(1)}, u32[]{:S(2)}, u32[]{:S(2)}) collective-permute-start(bf16[8,32,128]{2,1,0:T(8,128)(2,1)S(1)} %get-tuple-element.1201), channel_id=1, source_target_pairs={{4,0},{8,4},{12,8},{5,1},{9,5},{13,9},{6,2},{10,6},{14,10},{7,3},{... | collective-permute-start | bytes 196616 | tf_op jit(solution)/shard_map/while/body/eval_jaxpr/ppermute | solution.py:23
  69.7 4.4 %collective-permute-start.3 = (bf16[3,32,128]{2,1,0:T(8,128)(2,1)S(1)}, bf16[3,32,128]{2,1,0:T(8,128)(2,1)S(1)}, u32[]{:S(2)}, u32[]{:S(2)}) collective-permute-start(bf16[3,32,128]{2,1,0:T(8,128)(2,1)S(1)} %get-tuple-element.1102), channel_id=1, source_target_pairs={{1,0},{2,1},{3,2},{5,4},{6,5},{7,6},{9,8},{10,9},{11,10},{13,12},{... | collective-permute-start | bytes 73736 | tf_op jit(solution)/shard_map/while/body/eval_jaxpr/ppermute | solution.py:15
  71.6 5.1 %collective-permute-start.4 = (bf16[3,32,128]{2,1,0:T(8,128)(2,1)S(1)}, bf16[3,32,128]{2,1,0:T(8,128)(2,1)S(1)}, u32[]{:S(2)}, u32[]{:S(2)}) collective-permute-start(bf16[3,32,128]{2,1,0:T(8,128)(2,1)S(1)} %get-tuple-element.1103), channel_id=1, source_target_pairs={{0,1},{1,2},{2,3},{4,5},{5,6},{6,7},{8,9},{9,10},{10,11},{12,13},{... | collective-permute-start | bytes 73736 | tf_op jit(solution)/shard_map/while/body/eval_jaxpr/ppermute | solution.py:12
  76.8 6.2 %collective-permute-start.5 = (bf16[8,32,128]{2,1,0:T(8,128)(2,1)S(1)}, bf16[8,32,128]{2,1,0:T(8,128)(2,1)S(1)}, u32[]{:S(2)}, u32[]{:S(2)}) collective-permute-start(bf16[8,32,128]{2,1,0:T(8,128)(2,1)S(1)} %get-tuple-element.1201), channel_id=1, source_target_pairs={{4,0},{8,4},{12,8},{5,1},{9,5},{13,9},{6,2},{10,6},{14,10},{7,3},{... | collective-permute-start | bytes 196616 | tf_op jit(solution)/shard_map/while/body/eval_jaxpr/ppermute | solution.py:23
  83.0 4.4 %collective-permute-start.3 = (bf16[3,32,128]{2,1,0:T(8,128)(2,1)S(1)}, bf16[3,32,128]{2,1,0:T(8,128)(2,1)S(1)}, u32[]{:S(2)}, u32[]{:S(2)}) collective-permute-start(bf16[3,32,128]{2,1,0:T(8,128)(2,1)S(1)} %get-tuple-element.1102), channel_id=1, source_target_pairs={{1,0},{2,1},{3,2},{5,4},{6,5},{7,6},{9,8},{10,9},{11,10},{13,12},{... | collective-permute-start | bytes 73736 | tf_op jit(solution)/shard_map/while/body/eval_jaxpr/ppermute | solution.py:15
  84.9 5.1 %collective-permute-start.4 = (bf16[3,32,128]{2,1,0:T(8,128)(2,1)S(1)}, bf16[3,32,128]{2,1,0:T(8,128)(2,1)S(1)}, u32[]{:S(2)}, u32[]{:S(2)}) collective-permute-start(bf16[3,32,128]{2,1,0:T(8,128)(2,1)S(1)} %get-tuple-element.1103), channel_id=1, source_target_pairs={{0,1},{1,2},{2,3},{4,5},{5,6},{6,7},{8,9},{9,10},{10,11},{12,13},{... | collective-permute-start | bytes 73736 | tf_op jit(solution)/shard_map/while/body/eval_jaxpr/ppermute | solution.py:12
  90.2 11.2 %collective-permute-start.5 = (bf16[8,32,128]{2,1,0:T(8,128)(2,1)S(1)}, bf16[8,32,128]{2,1,0:T(8,128)(2,1)S(1)}, u32[]{:S(2)}, u32[]{:S(2)}) collective-permute-start(bf16[8,32,128]{2,1,0:T(8,128)(2,1)S(1)} %get-tuple-element.1201), channel_id=1, source_target_pairs={{4,0},{8,4},{12,8},{5,1},{9,5},{13,9},{6,2},{10,6},{14,10},{7,3},{... | collective-permute-start | bytes 196616 | tf_op jit(solution)/shard_map/while/body/eval_jaxpr/ppermute | solution.py:23
  101.4 0.7 copy-start.5
  102.0 4.4 %collective-permute-start = (bf16[3,32,128]{2,1,0:T(8,128)(2,1)S(1)}, bf16[3,32,128]{2,1,0:T(8,128)(2,1)S(1)}, u32[]{:S(2)}, u32[]{:S(2)}) collective-permute-start(bf16[3,32,128]{2,1,0:T(8,128)(2,1)S(1)} %get-tuple-element.1087), channel_id=1, source_target_pairs={{1,0},{2,1},{3,2},{5,4},{6,5},{7,6},{9,8},{10,9},{11,10},{13,12},{... | collective-permute-start | bytes 73736 | tf_op jit(solution)/shard_map/while/body/eval_jaxpr/ppermute | solution.py:15
  103.9 5.1 %collective-permute-start.1 = (bf16[3,32,128]{2,1,0:T(8,128)(2,1)S(1)}, bf16[3,32,128]{2,1,0:T(8,128)(2,1)S(1)}, u32[]{:S(2)}, u32[]{:S(2)}) collective-permute-start(bf16[3,32,128]{2,1,0:T(8,128)(2,1)S(1)} %get-tuple-element.1088), channel_id=1, source_target_pairs={{0,1},{1,2},{2,3},{4,5},{5,6},{6,7},{8,9},{9,10},{10,11},{12,13},{... | collective-permute-start | bytes 73736 | tf_op jit(solution)/shard_map/while/body/eval_jaxpr/ppermute | solution.py:12
  109.2 6.5 %collective-permute-start.2 = (bf16[8,32,128]{2,1,0:T(8,128)(2,1)S(1)}, bf16[8,32,128]{2,1,0:T(8,128)(2,1)S(1)}, u32[]{:S(2)}, u32[]{:S(2)}) collective-permute-start(bf16[8,32,128]{2,1,0:T(8,128)(2,1)S(1)} %get-tuple-element.1200), channel_id=1, source_target_pairs={{0,4},{4,8},{8,12},{1,5},{5,9},{9,13},{2,6},{6,10},{10,14},{3,7},{... | collective-permute-start | bytes 196616 | tf_op jit(solution)/shard_map/while/body/eval_jaxpr/ppermute | solution.py:23
  115.7 4.4 %collective-permute-start = (bf16[3,32,128]{2,1,0:T(8,128)(2,1)S(1)}, bf16[3,32,128]{2,1,0:T(8,128)(2,1)S(1)}, u32[]{:S(2)}, u32[]{:S(2)}) collective-permute-start(bf16[3,32,128]{2,1,0:T(8,128)(2,1)S(1)} %get-tuple-element.1087), channel_id=1, source_target_pairs={{1,0},{2,1},{3,2},{5,4},{6,5},{7,6},{9,8},{10,9},{11,10},{13,12},{... | collective-permute-start | bytes 73736 | tf_op jit(solution)/shard_map/while/body/eval_jaxpr/ppermute | solution.py:15
  117.6 5.1 %collective-permute-start.1 = (bf16[3,32,128]{2,1,0:T(8,128)(2,1)S(1)}, bf16[3,32,128]{2,1,0:T(8,128)(2,1)S(1)}, u32[]{:S(2)}, u32[]{:S(2)}) collective-permute-start(bf16[3,32,128]{2,1,0:T(8,128)(2,1)S(1)} %get-tuple-element.1088), channel_id=1, source_target_pairs={{0,1},{1,2},{2,3},{4,5},{5,6},{6,7},{8,9},{9,10},{10,11},{12,13},{... | collective-permute-start | bytes 73736 | tf_op jit(solution)/shard_map/while/body/eval_jaxpr/ppermute | solution.py:12
  122.8 11.5 %collective-permute-start.2 = (bf16[8,32,128]{2,1,0:T(8,128)(2,1)S(1)}, bf16[8,32,128]{2,1,0:T(8,128)(2,1)S(1)}, u32[]{:S(2)}, u32[]{:S(2)}) collective-permute-start(bf16[8,32,128]{2,1,0:T(8,128)(2,1)S(1)} %get-tuple-element.1200), channel_id=1, source_target_pairs={{0,4},{4,8},{8,12},{1,5},{5,9},{9,13},{2,6},{6,10},{10,14},{3,7},{... | collective-permute-start | bytes 196616 | tf_op jit(solution)/shard_map/while/body/eval_jaxpr/ppermute | solution.py:23
  134.3 4.4 %collective-permute-start = (bf16[3,32,128]{2,1,0:T(8,128)(2,1)S(1)}, bf16[3,32,128]{2,1,0:T(8,128)(2,1)S(1)}, u32[]{:S(2)}, u32[]{:S(2)}) collective-permute-start(bf16[3,32,128]{2,1,0:T(8,128)(2,1)S(1)} %get-tuple-element.1087), channel_id=1, source_target_pairs={{1,0},{2,1},{3,2},{5,4},{6,5},{7,6},{9,8},{10,9},{11,10},{13,12},{... | collective-permute-start | bytes 73736 | tf_op jit(solution)/shard_map/while/body/eval_jaxpr/ppermute | solution.py:15
  136.3 5.1 %collective-permute-start.1 = (bf16[3,32,128]{2,1,0:T(8,128)(2,1)S(1)}, bf16[3,32,128]{2,1,0:T(8,128)(2,1)S(1)}, u32[]{:S(2)}, u32[]{:S(2)}) collective-permute-start(bf16[3,32,128]{2,1,0:T(8,128)(2,1)S(1)} %get-tuple-element.1088), channel_id=1, source_target_pairs={{0,1},{1,2},{2,3},{4,5},{5,6},{6,7},{8,9},{9,10},{10,11},{12,13},{... | collective-permute-start | bytes 73736 | tf_op jit(solution)/shard_map/while/body/eval_jaxpr/ppermute | solution.py:12
  141.5 28.0 %collective-permute-start.2 = (bf16[8,32,128]{2,1,0:T(8,128)(2,1)S(1)}, bf16[8,32,128]{2,1,0:T(8,128)(2,1)S(1)}, u32[]{:S(2)}, u32[]{:S(2)}) collective-permute-start(bf16[8,32,128]{2,1,0:T(8,128)(2,1)S(1)} %get-tuple-element.1200), channel_id=1, source_target_pairs={{0,4},{4,8},{8,12},{1,5},{5,9},{9,13},{2,6},{6,10},{10,14},{3,7},{... | collective-permute-start | bytes 196616 | tf_op jit(solution)/shard_map/while/body/eval_jaxpr/ppermute | solution.py:23
  169.5 4.4 %collective-permute-start = (bf16[3,32,128]{2,1,0:T(8,128)(2,1)S(1)}, bf16[3,32,128]{2,1,0:T(8,128)(2,1)S(1)}, u32[]{:S(2)}, u32[]{:S(2)}) collective-permute-start(bf16[3,32,128]{2,1,0:T(8,128)(2,1)S(1)} %get-tuple-element.1087), channel_id=1, source_target_pairs={{1,0},{2,1},{3,2},{5,4},{6,5},{7,6},{9,8},{10,9},{11,10},{13,12},{... | collective-permute-start | bytes 73736 | tf_op jit(solution)/shard_map/while/body/eval_jaxpr/ppermute | solution.py:15
  171.4 5.1 %collective-permute-start.1 = (bf16[3,32,128]{2,1,0:T(8,128)(2,1)S(1)}, bf16[3,32,128]{2,1,0:T(8,128)(2,1)S(1)}, u32[]{:S(2)}, u32[]{:S(2)}) collective-permute-start(bf16[3,32,128]{2,1,0:T(8,128)(2,1)S(1)} %get-tuple-element.1088), channel_id=1, source_target_pairs={{0,1},{1,2},{2,3},{4,5},{5,6},{6,7},{8,9},{9,10},{10,11},{12,13},{... | collective-permute-start | bytes 73736 | tf_op jit(solution)/shard_map/while/body/eval_jaxpr/ppermute | solution.py:12
  178.6 0.9 copy-start.11
  179.5 1.1 copy-start.1
  179.5 1.2 copy-start.3
  181.3 0.8 copy-start.7
  181.3 0.8 copy-start.9
  184.0 6.2 %collective-permute-start.2 = (bf16[8,32,128]{2,1,0:T(8,128)(2,1)S(1)}, bf16[8,32,128]{2,1,0:T(8,128)(2,1)S(1)}, u32[]{:S(2)}, u32[]{:S(2)}) collective-permute-start(bf16[8,32,128]{2,1,0:T(8,128)(2,1)S(1)} %get-tuple-element.1200), channel_id=1, source_target_pairs={{0,4},{4,8},{8,12},{1,5},{5,9},{9,13},{2,6},{6,10},{10,14},{3,7},{... | collective-permute-start | bytes 196616 | tf_op jit(solution)/shard_map/while/body/eval_jaxpr/ppermute | solution.py:23
  190.2 4.4 %collective-permute-start = (bf16[3,32,128]{2,1,0:T(8,128)(2,1)S(1)}, bf16[3,32,128]{2,1,0:T(8,128)(2,1)S(1)}, u32[]{:S(2)}, u32[]{:S(2)}) collective-permute-start(bf16[3,32,128]{2,1,0:T(8,128)(2,1)S(1)} %get-tuple-element.1087), channel_id=1, source_target_pairs={{1,0},{2,1},{3,2},{5,4},{6,5},{7,6},{9,8},{10,9},{11,10},{13,12},{... | collective-permute-start | bytes 73736 | tf_op jit(solution)/shard_map/while/body/eval_jaxpr/ppermute | solution.py:15
  192.1 5.1 %collective-permute-start.1 = (bf16[3,32,128]{2,1,0:T(8,128)(2,1)S(1)}, bf16[3,32,128]{2,1,0:T(8,128)(2,1)S(1)}, u32[]{:S(2)}, u32[]{:S(2)}) collective-permute-start(bf16[3,32,128]{2,1,0:T(8,128)(2,1)S(1)} %get-tuple-element.1088), channel_id=1, source_target_pairs={{0,1},{1,2},{2,3},{4,5},{5,6},{6,7},{8,9},{9,10},{10,11},{12,13},{... | collective-permute-start | bytes 73736 | tf_op jit(solution)/shard_map/while/body/eval_jaxpr/ppermute | solution.py:12
  199.3 0.9 copy-start.11
  200.2 1.1 copy-start.1
  200.2 1.2 copy-start.3
  201.9 0.8 copy-start.7
  201.9 0.8 copy-start.9
  204.7 6.2 %collective-permute-start.2 = (bf16[8,32,128]{2,1,0:T(8,128)(2,1)S(1)}, bf16[8,32,128]{2,1,0:T(8,128)(2,1)S(1)}, u32[]{:S(2)}, u32[]{:S(2)}) collective-permute-start(bf16[8,32,128]{2,1,0:T(8,128)(2,1)S(1)} %get-tuple-element.1200), channel_id=1, source_target_pairs={{0,4},{4,8},{8,12},{1,5},{5,9},{9,13},{2,6},{6,10},{10,14},{3,7},{... | collective-permute-start | bytes 196616 | tf_op jit(solution)/shard_map/while/body/eval_jaxpr/ppermute | solution.py:23
  210.9 0.7 copy-start.4
where the time goes:
time: 213 us; the launch traced here: 212 us
  waiting for transfers between devices  88.5 us (42%)
  starting transfers between devices  87.2 us (41%)
  matrix products  21.6 us (10%)
  local copies, waits for them, and re-layouts  10.6 us (5%)
    ppermute x10, waiting for transfers between devices, shifted(): return lax.ppermute(shard, axis, pairs)  60.9 us
    ppermute x10, starting transfers between devices, shifted(): return lax.ppermute(shard, axis, pairs)  37.2 us
    ppermute x11, waiting for transfers between devices, with_halo(): lax.ppermute(lax.slice_in_dim(block, block.shape[dim] - width, None, axis...  26.8 us
    ppermute x11, starting transfers between devices, with_halo(): lax.ppermute(lax.slice_in_dim(block, block.shape[dim] - width, None, axis...  25.5 us
    ppermute x11, starting transfers between devices, with_halo(): lax.ppermute(lax.slice_in_dim(block, 0, width, axis=dim), axis, backward)  24.5 us
    dot_general x108, matrix products, conv_layer(): jnp.dot(window.reshape(row_count * col_count, window.shape[-1]), weight[o...  21.6 us
    squeeze x4, local copies, waits for them, and re-layouts, compute(): w_in[direction]  4.42 us
  transfers between devices with their start and end apart: 32, of which 21 were waited for; matrix products, arithmetic and copies ran while one was open for 1% of the time, Pallas kernels for 0%

commit v1 on v0

v1 whole, which is shorter than its diff:
```python
import functools

import jax
import jax.numpy as jnp
from jax import lax
from jax.experimental import pallas as pl
from jax.experimental.pallas import tpu as pltpu
from jax.sharding import PartitionSpec as P

HALO = 3


def activate(values):
    return 0.5 * values * (lax.erf(values * (0.5**0.5)) + 1.0)


def side_taps(values, cols):
    count = values.shape[0]
    col = lax.broadcasted_iota(jnp.int32, values.shape, 0) % cols
    left = jnp.where(col == 0, 0.0, pltpu.roll(values, 1, 0))
    right = jnp.where(col == cols - 1, 0.0, pltpu.roll(values, count - 1, 0))
    return jnp.concatenate([left, values, right], axis=1).astype(jnp.bfloat16)


def conv(values, weight, cols):
    taps = side_taps(values, cols)
    out = values.shape[0] - 2 * cols
    window = jnp.concatenate([taps[dy * cols : dy * cols + out] for dy in range(3)], axis=1)
    return jnp.dot(window, weight, preferred_element_type=jnp.float32)


def in_frame(values, first_row, total_rows, cols):
    row = first_row + lax.broadcasted_iota(jnp.int32, values.shape, 0) // cols
    return jnp.where((row >= 0) & (row < total_rows), values, 0.0)


def kernel(
    frames, rows_devices,
    feat, w_in, b_in, w_mid, b_mid, w_out, b_out,
    out_f, out_b,
    halo_feat, state, pre, result, wf, ws, wm, wo,
    load_sem, feat_send, feat_recv, send_sem, recv_sem, store_sem,
):
    t = lax.axis_index("frame")
    r = lax.axis_index("row")
    clips, _, rows, cols, ch = feat.shape
    total_rows = rows * rows_devices
    span = rows + 2 * HALO
    has_up, has_down = r > 0, r < rows_devices - 1

    loads = [
        pltpu.make_async_copy(feat.at[:, 0], halo_feat.at[:, HALO : HALO + rows], load_sem.at[0]),
        pltpu.make_async_copy(w_in.at[0, :, :, :ch], wf.at[:, :, :, :ch], load_sem.at[1]),
        pltpu.make_async_copy(w_in.at[1, :, :, :ch], wf.at[:, :, :, ch:], load_sem.at[2]),
        pltpu.make_async_copy(w_mid, wm, load_sem.at[3]),
        pltpu.make_async_copy(w_out, wo, load_sem.at[4]),
        pltpu.make_async_copy(w_in.at[:, :, :, ch:], ws, load_sem.at[5]),
    ]
    for load in loads:
        load.start()

    barrier = pltpu.get_barrier_semaphore()
    near = []
    for df in (-1, 0, 1):
        for dr in (-1, 0, 1):
            if df == 0 and dr == 0:
                continue
            tt, rr = t + df, r + dr
            ok = (tt >= 0) & (tt < frames) & (rr >= 0) & (rr < rows_devices)
            near.append((ok, tt, rr))
    for ok, tt, rr in near:
        @pl.when(ok)
        def _(tt=tt, rr=rr):
            pl.semaphore_signal(barrier, inc=1, device_id={"frame": tt, "row": rr})

    @pl.when(jnp.logical_not(has_up))
    def _():
        halo_feat[:, 0:HALO] = jnp.zeros((clips, HALO, cols, ch), jnp.bfloat16)
        state[:, :, 0:HALO] = jnp.zeros((2, clips, HALO, cols, ch), jnp.bfloat16)

    @pl.when(jnp.logical_not(has_down))
    def _():
        halo_feat[:, HALO + rows :] = jnp.zeros((clips, HALO, cols, ch), jnp.bfloat16)
        state[:, :, HALO + rows :] = jnp.zeros((2, clips, HALO, cols, ch), jnp.bfloat16)

    pl.semaphore_wait(barrier, sum(jnp.where(ok, 1, 0) for ok, _, _ in near))

    feat_up = pltpu.make_async_remote_copy(
        feat.at[:, 0, 0:HALO], halo_feat.at[:, HALO + rows :],
        feat_send.at[0], feat_recv.at[0], device_id={"row": r - 1},
    )
    feat_down = pltpu.make_async_remote_copy(
        feat.at[:, 0, rows - HALO :], halo_feat.at[:, 0:HALO],
        feat_send.at[1], feat_recv.at[1], device_id={"row": r + 1},
    )
    pl.when(has_up)(feat_up.start)
    pl.when(has_down)(feat_down.start)

    for load in loads[:3]:
        load.wait()
    pl.when(has_down)(feat_up.wait_recv)
    pl.when(has_up)(feat_down.wait_recv)

    weight_f = wf[...].reshape(9 * ch, 2 * ch)
    for clip in range(clips):
        field = halo_feat[clip].reshape(span * cols, ch).astype(jnp.float32)
        both = conv(field, weight_f, cols)
        for k in range(2):
            pre[k, clip] = both[:, k * ch : (k + 1) * ch] + b_in[k : k + 1, :]
    for load in loads[3:]:
        load.wait()

    first_dir = jnp.where(2 * t >= frames, 1, 0)

    def pieces(k, clip):
        target = t + 1 - 2 * k
        source = t - 1 + 2 * k
        going = (target >= 0) & (target < frames)
        coming = (source >= 0) & (source < frames)
        made = []
        for piece, (rows_from, rows_to, dr, sends, gets) in enumerate((
            (pl.ds(0, rows), pl.ds(HALO, rows), 0, going, coming),
            (pl.ds(0, HALO), pl.ds(HALO + rows, HALO), -1, going & has_up, coming & has_down),
            (pl.ds(rows - HALO, HALO), pl.ds(0, HALO), 1, going & has_down, coming & has_up),
        )):
            copy = pltpu.make_async_remote_copy(
                result.at[k, clip, rows_from], state.at[k, clip, rows_to],
                send_sem.at[k, clip, piece], recv_sem.at[k, clip, piece],
                device_id={"frame": target, "row": r + dr},
            )
            made.append((sends, gets, copy))
        return coming, made

    def step(index, carry):
        half = index // clips
        k = first_dir + half - 2 * first_dir * half
        clip = index % clips
        coming, made = pieces(k, clip)
        for _, gets, copy in made:
            pl.when(gets)(copy.wait_recv)

        @pl.when(coming)
        def _():
            field = state[k, clip].reshape(span * cols, ch).astype(jnp.float32)
            pre[k, clip] += conv(field, ws[k].reshape(9 * ch, ch), cols)

        top = r * rows
        first = in_frame(activate(pre[k, clip]), top - 2, total_rows, cols)
        first = first.astype(jnp.bfloat16).astype(jnp.float32)
        mid = conv(first, wm[k].reshape(9 * ch, ch), cols) + b_mid[pl.ds(k, 1), :]
        mid = in_frame(activate(mid), top - 1, total_rows, cols)
        last = conv(mid, wo[k].reshape(9 * ch, ch), cols) + b_out[pl.ds(k, 1), :]
        new = first[2 * cols : (2 + rows) * cols] + last
        result[k, clip] = new.astype(jnp.bfloat16).reshape(rows, cols, ch)
        for sends, _, copy in made:
            pl.when(sends)(copy.start)

        @pl.when(k == 0)
        def _():
            pltpu.make_async_copy(result.at[0, clip], out_f.at[clip, 0], store_sem.at[0, clip]).start()

        @pl.when(k == 1)
        def _():
            pltpu.make_async_copy(result.at[1, clip], out_b.at[clip, 0], store_sem.at[1, clip]).start()

        return carry

    lax.fori_loop(0, 2 * clips, step, 0)

    pl.when(has_up)(feat_up.wait_send)
    pl.when(has_down)(feat_down.wait_send)
    for k in range(2):
        for clip in range(clips):
            for sends, _, copy in pieces(k, clip)[1]:
                pl.when(sends)(copy.wait_send)
            out = (out_f, out_b)[k]
            pltpu.make_async_copy(result.at[k, clip], out.at[clip, 0], store_sem.at[k, clip]).wait()


def on_device(features, w_in, b_in, w_mid, b_mid, w_out, b_out):
    clips, own, rows, cols, ch = features.shape
    assert own == 1 and rows >= HALO
    span = rows + 2 * HALO
    bf16 = jnp.bfloat16
    anywhere = pl.BlockSpec(memory_space=pl.ANY)
    vmem = pl.BlockSpec(memory_space=pltpu.VMEM)
    return pl.pallas_call(
        functools.partial(kernel, lax.axis_size("frame"), lax.axis_size("row")),
        out_shape=[jax.ShapeDtypeStruct(features.shape, bf16)] * 2,
        in_specs=[anywhere, anywhere, vmem, anywhere, vmem, anywhere, vmem],
        out_specs=[anywhere, anywhere],
        scratch_shapes=[
            pltpu.VMEM((clips, span, cols, ch), bf16),
            pltpu.VMEM((2, clips, span, cols, ch), bf16),
            pltpu.VMEM((2, clips, (rows + 4) * cols, ch), jnp.float32),
            pltpu.VMEM((2, clips, rows, cols, ch), bf16),
            pltpu.VMEM((3, 3, ch, 2 * ch), bf16),
            pltpu.VMEM((2, 3, 3, ch, ch), bf16),
            pltpu.VMEM((2, 3, 3, ch, ch), bf16),
            pltpu.VMEM((2, 3, 3, ch, ch), bf16),
            pltpu.SemaphoreType.DMA((6,)),
            pltpu.SemaphoreType.DMA((2,)),
            pltpu.SemaphoreType.DMA((2,)),
            pltpu.SemaphoreType.DMA((2, clips, 3)),
            pltpu.SemaphoreType.DMA((2, clips, 3)),
            pltpu.SemaphoreType.DMA((2, clips)),
        ],
        compiler_params=pltpu.CompilerParams(
            collective_id=0, has_side_effects=True, vmem_limit_bytes=32 * 1024 * 1024
        ),
    )(features, w_in, b_in, w_mid, b_mid, w_out, b_out)


def solution(mesh):
    split = P("parts", "frame", "row", None, None)
    return jax.shard_map(
        on_device,
        mesh=mesh,
        in_specs=(split, P(), P(), P(), P(), P(), P()),
        out_specs=(split, split),
        check_vma=False,
    )
```

time: 213 us -> 37.2 us (0.17)
  the two profiles are of different devices: /device:TPU:26 before, /device:TPU:1 now
where the time goes in v1:
time: 37.2 us; the launch traced here: 36.9 us
  Pallas kernels  28.6 us (77%)
  local copies, waits for them, and re-layouts  7.64 us (21%)
  between operations  0.66 us (2%)
    pallas_call x1, Pallas kernels, on_device(): pl.pallas_call(functools.partial(kernel, lax.axis_size('frame'), lax.axis...  28.6 us
    unnamed x16, local copies, waits for them, and re-layouts  7.64 us

profile of v1, /device:TPU:1, one launch (start us, length us, event | category | flops | bytes accessed | tf_op | source)
XLA Modules:
  0.0 36.9 jit_solution(5553597601996110552)
XLA Ops:
  0.6 0.0 copy-start
  0.6 1.3 %copy-done = bf16[2,3,3,256,128]{4,3,2,1,0:T(8,128)(2,1)S(1)} copy-done((bf16[2,3,3,256,128]{4,3,2,1,0:T(8,128)(2,1)S(1)}, bf16[2,3,3,256,128]{4,3,2,1,0:T(8,128)(2,1)}, u32[]{:S(2)}) %copy-start) | copy-done | bytes 1179672
  1.9 0.0 copy-start.1
  1.9 1.1 %copy-done.1 = bf16[2,3,3,128,128]{4,3,2,1,0:T(8,128)(2,1)S(1)} copy-done((bf16[2,3,3,128,128]{4,3,2,1,0:T(8,128)(2,1)S(1)}, bf16[2,3,3,128,128]{4,3,2,1,0:T(8,128)(2,1)}, u32[]{:S(2)}) %copy-start.1) | copy-done | bytes 589848
  3.0 0.0 copy-start.2
  3.0 1.1 %copy-done.2 = bf16[2,3,3,128,128]{4,3,2,1,0:T(8,128)(2,1)S(1)} copy-done((bf16[2,3,3,128,128]{4,3,2,1,0:T(8,128)(2,1)S(1)}, bf16[2,3,3,128,128]{4,3,2,1,0:T(8,128)(2,1)}, u32[]{:S(2)}) %copy-start.2) | copy-done | bytes 589848
  4.0 0.0 copy-start.3
  4.0 0.9 %copy-done.3 = bf16[2,1,8,32,128]{4,3,2,1,0:T(8,128)(2,1)S(1)} copy-done((bf16[2,1,8,32,128]{4,3,2,1,0:T(8,128)(2,1)S(1)}, bf16[2,1,8,32,128]{4,3,2,1,0:T(8,128)(2,1)}, u32[]{:S(2)}) %copy-start.3) | copy-done | bytes 131096
  4.9 0.0 copy-start.4
  4.9 0.7 %copy-done.4 = f32[2,128]{1,0:T(2,128)S(1)} copy-done((f32[2,128]{1,0:T(2,128)S(1)}, f32[2,128]{1,0:T(2,128)}, u32[]{:S(2)}) %copy-start.4) | copy-done | bytes 1048
  5.6 0.0 copy-start.5
  5.6 0.7 %copy-done.5 = f32[2,128]{1,0:T(2,128)S(1)} copy-done((f32[2,128]{1,0:T(2,128)S(1)}, f32[2,128]{1,0:T(2,128)}, u32[]{:S(2)}) %copy-start.5) | copy-done | bytes 1048
  6.3 0.0 copy-start.6
  6.3 0.7 %copy-done.6 = f32[2,128]{1,0:T(2,128)S(1)} copy-done((f32[2,128]{1,0:T(2,128)S(1)}, f32[2,128]{1,0:T(2,128)}, u32[]{:S(2)}) %copy-start.6) | copy-done | bytes 1048
  7.0 28.6 %shard_map.86 = (bf16[2,1,8,32,128]{4,3,2,1,0:T(8,128)(2,1)S(1)}, bf16[2,1,8,32,128]{4,3,2,1,0:T(8,128)(2,1)S(1)}) custom-call(bf16[2,1,8,32,128]{4,3,2,1,0:T(8,128)(2,1)S(1)} %copy-done.3, bf16[2,3,3,256,128]{4,3,2,1,0:T(8,128)(2,1)S(1)} %copy-done, f32[2,128]{1,0:T(2,128)S(1)} %copy-done.4, bf16[2,3,3,128,128]{4,3,2,1,0:T(8,128)(2,1)S(1)} %copy-done.1, ...), custom_call_target="tpu_custom_call" | custom-call | tf_op jit(solution)/shard_map/pallas_call | solution.py:187
  35.6 0.7 %copy.11 = bf16[2,1,8,32,128]{4,3,2,1,0:T(8,128)(2,1)} copy(bf16[2,1,8,32,128]{4,3,2,1,0:T(8,128)(2,1)S(1)} %get-tuple-element.4) | data formatting | bytes 262144
  36.2 0.7 %copy.12 = bf16[2,1,8,32,128]{4,3,2,1,0:T(8,128)(2,1)} copy(bf16[2,1,8,32,128]{4,3,2,1,0:T(8,128)(2,1)S(1)} %get-tuple-element.5) | data formatting | bytes 262144
Async XLA Ops:
  0.6 1.3 %copy-start = (bf16[2,3,3,256,128]{4,3,2,1,0:T(8,128)(2,1)S(1)}, bf16[2,3,3,256,128]{4,3,2,1,0:T(8,128)(2,1)}, u32[]{:S(2)}) copy-start(bf16[2,3,3,256,128]{4,3,2,1,0:T(8,128)(2,1)} %w_in.1) | copy-start | bytes 3538948
  1.9 1.1 %copy-start.1 = (bf16[2,3,3,128,128]{4,3,2,1,0:T(8,128)(2,1)S(1)}, bf16[2,3,3,128,128]{4,3,2,1,0:T(8,128)(2,1)}, u32[]{:S(2)}) copy-start(bf16[2,3,3,128,128]{4,3,2,1,0:T(8,128)(2,1)} %w_mid.1) | copy-start | bytes 1769476
  3.0 1.1 %copy-start.2 = (bf16[2,3,3,128,128]{4,3,2,1,0:T(8,128)(2,1)S(1)}, bf16[2,3,3,128,128]{4,3,2,1,0:T(8,128)(2,1)}, u32[]{:S(2)}) copy-start(bf16[2,3,3,128,128]{4,3,2,1,0:T(8,128)(2,1)} %w_out.1) | copy-start | bytes 1769476
  4.0 0.9 %copy-start.3 = (bf16[2,1,8,32,128]{4,3,2,1,0:T(8,128)(2,1)S(1)}, bf16[2,1,8,32,128]{4,3,2,1,0:T(8,128)(2,1)}, u32[]{:S(2)}) copy-start(bf16[2,1,8,32,128]{4,3,2,1,0:T(8,128)(2,1)} %feat.1) | copy-start | bytes 393220
  4.9 0.7 %copy-start.4 = (f32[2,128]{1,0:T(2,128)S(1)}, f32[2,128]{1,0:T(2,128)}, u32[]{:S(2)}) copy-start(f32[2,128]{1,0:T(2,128)} %b_in.1) | copy-start | bytes 3076
  5.6 0.7 %copy-start.5 = (f32[2,128]{1,0:T(2,128)S(1)}, f32[2,128]{1,0:T(2,128)}, u32[]{:S(2)}) copy-start(f32[2,128]{1,0:T(2,128)} %b_mid.1) | copy-start | bytes 3076
  6.3 0.7 %copy-start.6 = (f32[2,128]{1,0:T(2,128)S(1)}, f32[2,128]{1,0:T(2,128)}, u32[]{:S(2)}) copy-start(f32[2,128]{1,0:T(2,128)} %b_out.1) | copy-start | bytes 3076
